TPU v7x, 256 devices: a whole 4x4x8 slice. The times are simulated.
256 devices in a mesh: prow: 16 (over x, y), pcol: 16 (over z, core).
Axes of the slice: x: 4, y: 4, z: 8, core: 2. Of those that a mesh axis runs over, the one named last changes fastest.
Arguments:
- inverse_tiles: float32 [24576, 24576], P('prow', 'pcol'), may hold values from -6 to 6
- factor_rows: float32 [24576, 512], P('prow'), may hold values from -0.0390625 to 0.0390625
- diag_inverse: float32 [512, 512], P('prow', 'pcol'), may hold values from -6 to 6
- pattern: int32 [192], replicated, may hold values from 0 to 1, as said below
Outputs:
- column_block: float32 [24576, 512], P(('prow', 'pcol'))
- diagonal_block: float32 [512, 512], P('prow', 'pcol')
Inputs may be any that keep to these rules, and one draw needn't show every extreme that they name: `pattern`: 1 where the block of ancestor rows lies in the supernode's structure, else 0; the first block always lies in it and the last never.
All inputs are finite; a program needn't handle non-finite values.
Results may differ from a plain program's by a relative error of at most 0.000078.
Values sent between devices are 32-bit elements; how exact they have to be, the bound alone decides.
A program may use at most 64 MiB of HBM per device.

v0:
```python
import jax
import jax.numpy as jnp
from jax import lax
from jax.sharding import PartitionSpec as P

BLK = 128


def broadcast(shard, axis, root):
    mine = lax.axis_index(axis) == root
    return lax.psum(jnp.where(mine, shard, jnp.zeros_like(shard)), axis)


def row_select(pattern, first_row, row_count):
    global_rows = first_row + lax.iota(jnp.int32, row_count)
    block_ids = global_rows // BLK
    blocks = lax.iota(jnp.int32, pattern.shape[0])
    match = block_ids[:, None] == blocks[None, :]
    return jnp.sum(jnp.where(match, pattern[None, :], 0), axis=1).astype(jnp.float32)


def local(inverse_tiles, factor_rows, diag_inverse, pattern):
    n_row = lax.axis_size("prow")
    n_col = lax.axis_size("pcol")
    row_index = lax.axis_index("prow")
    col_index = lax.axis_index("pcol")
    tile_rows = inverse_tiles.shape[0]
    width = factor_rows.shape[1]
    col_ratio = n_col // n_row
    tile_mask = row_select(pattern, row_index * tile_rows, tile_rows)
    masked_rows = factor_rows * tile_mask[:, None]
    root_index = col_index // col_ratio
    column_factor = broadcast(masked_rows, "prow", root_index)
    out_rows = tile_rows // n_col
    own_mask = lax.dynamic_slice_in_dim(tile_mask, col_index * out_rows, out_rows, 0)
    summed = lax.psum_scatter(
        jnp.dot(
            inverse_tiles,
            column_factor,
            precision=lax.Precision.HIGHEST,
            preferred_element_type=jnp.float32,
        ),
        "pcol",
        scatter_dimension=0,
        tiled=True,
    )
    column_block = -summed * own_mask[:, None]
    own_factor = lax.dynamic_slice_in_dim(masked_rows, col_index * out_rows, out_rows, 0)
    correction = jnp.dot(
        own_factor.T,
        column_block,
        precision=lax.Precision.HIGHEST,
        preferred_element_type=jnp.float32,
    )
    share_rows = width // n_row
    share_cols = width // n_col
    total = lax.psum(correction, ("prow", "pcol"))
    mine = lax.dynamic_slice_in_dim(total, row_index * share_rows, share_rows, 0)
    mine = lax.dynamic_slice_in_dim(mine, col_index * share_cols, share_cols, 1)
    diagonal_block = diag_inverse - mine
    return (column_block, diagonal_block)


def solution(mesh):
    return jax.shard_map(
        local,
        mesh=mesh,
        in_specs=(P("prow", "pcol"), P("prow", None), P("prow", "pcol"), P()),
        out_specs=(P(("prow", "pcol"), None), P("prow", "pcol")),
        check_vma=False,
    )
```

profile of v0, /device:TPU:2, one launch (start us, length us, event | category | flops | bytes accessed | tf_op | source)
XLA Modules:
  0.0 486.7 jit_solution(2618782349382456584)
XLA Ops:
  7.2 0.0 all-reduce.3.cloned.1.call-start
  7.2 0.9 select_reduce_fusion
  8.2 4.1 broadcast_select_fusion
  12.2 0.0 all-reduce.3.cloned.1.call-update
  12.3 0.0 reduce-scatter.4.cloned.1.call-start
  12.3 108.1 %all-reduce.3.cloned.1.call-done = f32[1536,512]{1,0:T(8,128)} async-done(((f32[1536,512]{1,0:T(8,128)}), f32[1536,512]{1,0:T(8,128)}) %all-reduce.3.cloned.1.call-update) | async-done | bytes 3145744 | tf_op jit(solution)/shard_map/psum | solution.py:11
  120.4 33.8 %convolution_bitcast_fusion = f32[1536,512]{0,1:T(8,128)} fusion(f32[1536,512]{1,0:T(8,128)} %all-reduce.3.cloned.1.call-done, f32[1536,1536]{1,0:T(8,128)} %param.4), kind=kOutput, calls=%fused_computation | convolution fusion | flops 14495514624 | bytes 15728640 | tf_op jit(solution)/shard_map/dot_general | solution.py:37
  154.1 3.5 copy.9
  157.7 0.0 copy-start
  157.7 0.0 reduce-scatter.4.cloned.1.call-update
  157.7 0.0 all-reduce.5.cloned.1.call-start
  157.8 0.1 dynamic_slice.10
  157.9 61.0 %reduce-scatter.4.cloned.1.call-done = f32[96,512]{1,0:T(8,128)} async-done(((f32[1536,512]{1,0:T(8,128)}), f32[96,512]{1,0:T(8,128)}) %reduce-scatter.4.cloned.1.call-update) | async-done | bytes 196624
  218.8 1.8 copy.10
  220.6 1.0 negate_multiply_fusion
  221.6 2.1 fusion
  223.6 0.0 all-reduce.5.cloned.1.call-update
  223.7 0.8 copy.8
  224.5 254.3 %all-reduce.5.cloned.1.call-done = f32[512,512]{1,0:T(8,128)} async-done(((f32[512,512]{1,0:T(8,128)}), f32[512,512]{1,0:T(8,128)}) %all-reduce.5.cloned.1.call-update) | async-done | bytes 1048592 | tf_op jit(solution)/shard_map/psum | solution.py:57
  478.8 0.0 copy-done
  478.8 1.5 dynamic-slice_subtract_fusion
  (2 shorter events, 0.0 us)
Async XLA Ops:
  7.2 113.2 %all-reduce.3.cloned.1.call-start = ((), (), s32[]{:S(2)}) async-start(), calls=%async_computation.1 | async-start | bytes 6291456 | tf_op jit(solution)/shard_map/psum | solution.py:11
  12.3 206.6 %reduce-scatter.4.cloned.1.call-start = ((), (), s32[]{:S(2)}) async-start(), calls=%async_computation.3 | async-start | bytes 3342336
  157.7 321.1 %copy-start = (f32[32,32]{1,0:T(8,128)S(1)}, f32[32,32]{1,0:T(8,128)}, u32[]{:S(2)}) copy-start(f32[32,32]{1,0:T(8,128)} %param.6) | copy-start | bytes 12292
  157.7 321.0 %all-reduce.5.cloned.1.call-start = ((), (), s32[]{:S(2)}) async-start(), calls=%async_computation.2 | async-start | bytes 2097152 | tf_op jit(solution)/shard_map/psum | solution.py:57
Sparse Core Ops, SparseCore 0:
  12.4 107.9 all-reduce.2
  157.8 60.9 reduce-scatter.3
  224.3 254.4 all-reduce.4
where the time goes:
time: 487 us
  waiting for transfers between devices  423 us (87%)
  matrix products  35.8 us (7%)
  between operations  13.8 us (3%)
  other arithmetic  7.43 us (2%)
  local copies, waits for them, and re-layouts  6.18 us (1%)
    psum x1, waiting for transfers between devices, local(): total = lax.psum(correction, ('prow', 'pcol'))  254 us
    psum x1, waiting for transfers between devices, broadcast(): return lax.psum(jnp.where(mine, shard, jnp.zeros_like(shard)), axis)  108 us
    unnamed x4, waiting for transfers between devices  61 us
    dot_general x1, matrix products, local(): jnp.dot(inverse_tiles, column_factor, precision=lax.Precision.HIGHEST, pr...  33.8 us
  transfers between devices with their start and end apart: 3, of which 3 were waited for; matrix products, arithmetic and copies ran while one was open for 0% of the time, Pallas kernels for 0%

commit v1 on v0

--- a/solution.py
+++ b/solution.py
@@ -54,7 +54,8 @@
     )
     share_rows = width // n_row
     share_cols = width // n_col
-    total = lax.psum(correction, ("prow", "pcol"))
+    half = lax.psum(correction, "pcol")
+    total = lax.psum(half, "prow")
     mine = lax.dynamic_slice_in_dim(total, row_index * share_rows, share_rows, 0)
     mine = lax.dynamic_slice_in_dim(mine, col_index * share_cols, share_cols, 1)
     diagonal_block = diag_inverse - mine

time: 487 us -> 443 us (0.910)
  waiting for transfers between devices: 423 us -> 379 us
    psum x1 -> x2, waiting for transfers between devices: 254 us -> 210 us  [the longest x1 110 us: local(): half = lax.psum(correction, 'pcol')]
    unnamed x4 -> x5, waiting for transfers between devices: 61 us -> 61 us
  transfers between devices with their start and end apart: 3 -> 4, of which waited for: 3 -> 4; matrix products, arithmetic and copies ran while one was open for 0% -> 0% of each run, Pallas kernels for 0% -> 0%
where the time goes in v1:
time: 443 us; the launch traced here: 442 us
  waiting for transfers between devices  379 us (86%)
  matrix products  35.8 us (8%)
  between operations  13.8 us (3%)
  other arithmetic  7.43 us (2%)
  local copies, waits for them, and re-layouts  6.19 us (1%)
    psum x1, waiting for transfers between devices, local(): half = lax.psum(correction, 'pcol')  110 us
    psum x1, waiting for transfers between devices, broadcast(): return lax.psum(jnp.where(mine, shard, jnp.zeros_like(shard)), axis)  108 us
    psum x1, waiting for transfers between devices, local(): total = lax.psum(half, 'prow')  99.6 us
    unnamed x5, waiting for transfers between devices  61 us
    dot_general x1, matrix products, local(): jnp.dot(inverse_tiles, column_factor, precision=lax.Precision.HIGHEST, pr...  33.8 us
  transfers between devices with their start and end apart: 4, of which 4 were waited for; matrix products, arithmetic and copies ran while one was open for 0% of the time, Pallas kernels for 0%

profile of v1, /device:TPU:2, one launch (start us, length us, event | category | flops | bytes accessed | tf_op | source)
XLA Modules:
  0.0 442.3 jit_solution(2130751619566210688)
XLA Ops:
  7.2 0.0 all-reduce.4.cloned.1.call-start
  7.2 0.9 select_reduce_fusion
  8.2 4.1 broadcast_select_fusion
  12.2 0.0 all-reduce.4.cloned.1.call-update
  12.3 0.0 reduce-scatter.4.cloned.1.call-start
  12.3 108.1 %all-reduce.4.cloned.1.call-done = f32[1536,512]{1,0:T(8,128)} async-done(((f32[1536,512]{1,0:T(8,128)}), f32[1536,512]{1,0:T(8,128)}) %all-reduce.4.cloned.1.call-update) | async-done | bytes 3145744 | tf_op jit(solution)/shard_map/psum | solution.py:11
  120.4 33.8 %convolution_bitcast_fusion = f32[1536,512]{0,1:T(8,128)} fusion(f32[1536,512]{1,0:T(8,128)} %all-reduce.4.cloned.1.call-done, f32[1536,1536]{1,0:T(8,128)} %param.4), kind=kOutput, calls=%fused_computation | convolution fusion | flops 14495514624 | bytes 15728640 | tf_op jit(solution)/shard_map/dot_general | solution.py:37
  154.1 3.5 copy.9
  157.7 0.0 reduce-scatter.4.cloned.1.call-update
  157.7 0.0 copy-start
  157.7 0.0 all-reduce.6.cloned.1.call-start
  157.8 0.1 dynamic_slice.10
  157.9 61.0 %reduce-scatter.4.cloned.1.call-done = f32[96,512]{1,0:T(8,128)} async-done(((f32[1536,512]{1,0:T(8,128)}), f32[96,512]{1,0:T(8,128)}) %reduce-scatter.4.cloned.1.call-update) | async-done | bytes 196624
  218.8 1.8 copy.10
  220.6 1.0 negate_multiply_fusion
  221.6 2.1 fusion
  223.6 0.0 all-reduce.6.cloned.1.call-update
  223.7 0.0 all-reduce.8.cloned.1.call-start
  223.7 110.2 %all-reduce.6.cloned.1.call-done = f32[512,512]{1,0:T(8,128)} async-done(((f32[512,512]{1,0:T(8,128)}), f32[512,512]{1,0:T(8,128)}) %all-reduce.6.cloned.1.call-update) | async-done | bytes 1048592 | tf_op jit(solution)/shard_map/psum | solution.py:57
  333.9 0.0 all-reduce.8.cloned.1.call-update
  333.9 0.8 copy.8
  334.8 99.6 %all-reduce.8.cloned.1.call-done = f32[512,512]{1,0:T(8,128)} async-done(((f32[512,512]{1,0:T(8,128)}), f32[512,512]{1,0:T(8,128)}) %all-reduce.8.cloned.1.call-update) | async-done | bytes 1048592 | tf_op jit(solution)/shard_map/psum | solution.py:58
  434.3 0.0 copy-done
  434.3 1.5 dynamic-slice_subtract_fusion
  (2 shorter events, 0.0 us)
Async XLA Ops:
  7.2 113.2 %all-reduce.4.cloned.1.call-start = ((), (), s32[]{:S(2)}) async-start(), calls=%async_computation.1 | async-start | bytes 6291456 | tf_op jit(solution)/shard_map/psum | solution.py:11
  12.3 206.6 %reduce-scatter.4.cloned.1.call-start = ((), (), s32[]{:S(2)}) async-start(), calls=%async_computation.4 | async-start | bytes 3342336
  157.7 276.6 %copy-start = (f32[32,32]{1,0:T(8,128)S(1)}, f32[32,32]{1,0:T(8,128)}, u32[]{:S(2)}) copy-start(f32[32,32]{1,0:T(8,128)} %param.6) | copy-start | bytes 12292
  157.7 176.2 %all-reduce.6.cloned.1.call-start = ((), (), s32[]{:S(2)}) async-start(), calls=%async_computation.2 | async-start | bytes 2097152 | tf_op jit(solution)/shard_map/psum | solution.py:57
  223.7 210.7 %all-reduce.8.cloned.1.call-start = ((), (), s32[]{:S(2)}) async-start(), calls=%async_computation.3 | async-start | bytes 2097152 | tf_op jit(solution)/shard_map/psum | solution.py:58
Sparse Core Ops, SparseCore 0:
  12.4 107.9 all-reduce.3
  157.8 60.9 reduce-scatter.3
  223.8 110.0 all-reduce.5
  337.4 96.9 all-reduce.7
